TPU v7x, 32 devices: a whole 2x2x4 slice. The times are simulated.
32 devices in a mesh: genome: 8 (over y, x, core), sample: 4 (over z).
Axes of the slice: x: 2, y: 2, z: 4, core: 2. Of those that a mesh axis runs over, the one named last changes fastest.
Arguments:
- genotypes: bfloat16 [32768, 4096], P('sample', 'genome'), may hold values from 0 to 2
- probes: bfloat16 [32768, 1024], P('sample', 'genome'), may hold values from -12 to 12
- covariates: float32 [20, 32768], P(None, 'sample')
- probe_locus: int32 [1024], replicated, may hold values from 0 to 39999, as said below
- probe_counts: int32 [8], replicated, may hold values from 32 to 128, as said below
- reach: int32 [8], P('genome'), may hold values from 1 to 2, as said below
- positions: int32 [4096], P(('genome', 'sample')), may hold values from 0 to 39999, as said below
Outputs:
- zscores: float32 [4096, 640], P(('genome', 'sample'))
Inputs may be any that keep to these rules, and one draw needn't show every extreme that they name: `probe_locus`: slot q of block b has a position in b * 5000 to (b + 1) * 5000 - 1. `probe_counts`: some block holds exactly 128. `reach`: some block reaches exactly 2. `positions`: variants of block b lie in b * 5000 to (b + 1) * 5000 - 1.
All inputs are finite; a program needn't handle non-finite values.
Results may differ from a plain program's by a relative error of at most 0.0041.
Values may be sent and summed in bfloat16 or wider, within the bound.
A program may use at most 128 MiB of HBM per device.

v0:
```python
import jax
import jax.numpy as jnp
from jax import lax
from jax.sharding import PartitionSpec as P

REACH = 2
WIN = 10000


def from_behind(value, axis, steps):
    count = lax.axis_size(axis)
    first, last = (max(0, -steps), min(count, count - steps))
    return lax.ppermute(value, axis, [(source, source + steps) for source in range(first, last)])


def fitted_part(data, basis, coef_sum, factor):
    coef = jax.scipy.linalg.cho_solve((factor, True), coef_sum)
    fitted = jnp.dot(basis.T, coef, precision=lax.Precision.HIGHEST)
    return (data.astype(jnp.float32) - fitted).astype(jnp.bfloat16)


def variant_products(left, right):
    return lax.dot_general(
        left, right, (((0,), (0,)), ((), ())), preferred_element_type=jnp.float32
    )


def local(genotypes, probes, covariates, probe_locus, probe_counts, reach, positions):
    rows = genotypes.shape[0]
    width_v = genotypes.shape[1]
    width_p = probes.shape[1]
    ncov = covariates.shape[0]
    nblk = probe_counts.shape[0]
    wide = (2 * REACH + 1) * width_p
    basis = jnp.concatenate([jnp.ones((1, rows), jnp.float32), covariates], 0)
    gram = jnp.dot(basis, basis.T, precision=lax.Precision.HIGHEST)
    cross_geno = jnp.dot(basis, genotypes.astype(jnp.float32), precision=lax.Precision.HIGHEST)
    cross_probe = jnp.dot(basis, probes.astype(jnp.float32), precision=lax.Precision.HIGHEST)
    gram, cross_geno, cross_probe = lax.psum((gram, cross_geno, cross_probe), "sample")
    factor = jnp.linalg.cholesky(gram)
    geno_res = fitted_part(genotypes, basis, cross_geno, factor)
    probe_res = fitted_part(probes, basis, cross_probe, factor)
    pieces = {0: probe_res}
    for direction in (1, -1):
        current = probe_res
        for stepper in range(1, REACH + 1):
            current = from_behind(current, "genome", -direction)
            pieces[direction * stepper] = current
    window = jnp.concatenate([pieces[offset] for offset in range(-REACH, REACH + 1)], 1)
    gres32 = geno_res.astype(jnp.float32)
    win32 = window.astype(jnp.float32)
    gnorm, pnorm = lax.psum((jnp.sum(gres32 * gres32, 0), jnp.sum(win32 * win32, 0)), "sample")
    share = width_v // lax.axis_size("sample")
    first_row = lax.axis_index("sample") * share
    total = lax.psum(variant_products(geno_res, window), "sample")
    mine = lax.dynamic_slice_in_dim(total, first_row, share, 0)
    gnorm_mine = lax.dynamic_slice_in_dim(gnorm, first_row, share, 0)
    block = lax.axis_index("genome")
    column = jnp.arange(wide, dtype=jnp.int32)
    offset_of = column // width_p - REACH
    slot_of = column % width_p
    padded_start = jnp.pad(probe_locus, (REACH * width_p, REACH * width_p))
    padded_count = jnp.pad(probe_counts, (REACH, REACH))
    starts = lax.dynamic_slice_in_dim(padded_start, block * width_p, wide, 0)
    counted = lax.dynamic_slice_in_dim(padded_count, block, 2 * REACH + 1, 0)[column // width_p]
    inside = (block + offset_of >= 0) & (block + offset_of < nblk)
    tested = inside & (slot_of < counted) & (jnp.abs(offset_of) <= reach[0])
    tested = tested[None, :] & (jnp.abs(positions[:, None] - starts[None, :]) <= WIN)
    samples = rows * lax.axis_size("sample")
    scale = jnp.sqrt(jnp.float32(samples - ncov - 2))
    value = (
        scale * mine / (jnp.sqrt(gnorm_mine + 1e-06)[:, None] * jnp.sqrt(pnorm + 1e-06)[None, :])
    )
    return jnp.where(tested, value, jnp.float32(0.0))


def solution(mesh):
    placed = (
        P("sample", "genome"),
        P("sample", "genome"),
        P(None, "sample"),
        P(),
        P(),
        P("genome"),
        P(("genome", "sample")),
    )
    return jax.shard_map(
        local, mesh=mesh, in_specs=placed, out_specs=P(("genome", "sample"), None), check_vma=False
    )
```

profile of v0, /device:TPU:0, one launch (start us, length us, event | category | flops | bytes accessed | tf_op | source)
XLA Modules:
  0.0 238.4 jit_solution(11219489892866472697)
XLA Ops:
  6.5 0.0 copy-start.1
  6.5 0.0 all-reduce.7.cloned.1.call-start
  6.5 2.4 %fusion.7 = f32[21,21]{0,1:T(8,128)S(1)} fusion(f32[20,8192]{1,0:T(8,128)} %param.9), kind=kOutput, calls=%fused_computation.11 | convolution fusion | flops 43352064 | bytes 657124 | tf_op jit(solution)/shard_map/dot_general | solution.py:36
  9.0 2.8 %fusion.2 = f32[21,128]{1,0:T(8,128)S(1)} fusion(bf16[8192,128]{1,0:T(8,128)(2,1)} %param.8, f32[20,8192]{1,0:T(8,128)} %param.9), kind=kOutput, calls=%fused_computation.6 | convolution fusion | flops 264241152 | bytes 2763264 | tf_op jit(solution)/shard_map/dot_general | solution.py:38
  11.8 0.0 copy-start.4
  11.8 0.0 copy-start.2
  11.8 4.1 %copy.13 = bf16[8192,128]{0,1:T(8,128)(2,1)} copy(bf16[8192,128]{1,0:T(8,128)(2,1)} %param.8) | data formatting | bytes 4194304 | tf_op args[1]
  15.9 0.0 copy-done.1
  15.9 5.9 %fusion.5 = f32[21,512]{1,0:T(8,128)S(1)} fusion(bf16[8192,512]{1,0:T(8,128)(2,1)} %param.7, f32[20,8192]{1,0:T(8,128)S(1)} %copy-done.1), kind=kOutput, calls=%fused_computation.9 | convolution fusion | flops 1056964608 | bytes 9086976 | tf_op jit(solution)/shard_map/dot_general | solution.py:37
  21.8 22.0 %all-reduce.4 = (f32[21,512]{1,0:T(8,128)S(1)}, f32[21,21]{0,1:T(8,128)S(1)}, f32[21,128]{1,0:T(8,128)S(1)}) all-reduce(f32[21,512]{1,0:T(8,128)S(1)} %fusion.5, f32[21,21]{0,1:T(8,128)S(1)} %fusion.7, f32[21,128]{1,0:T(8,128)S(1)} %fusion.2), channel_id=1, replica_groups=mesh['genome'=8,'sample'=4] {'sample'}, use_global_device_ids=true, to_apply=%region_3.4 | all-reduce | flops 13881 | bytes 111048 | tf_op jit(solution)/shard_map/psum | solution.py:39
  43.9 0.1 copy.12
  44.0 1.9 cholesky.16
  45.9 0.6 compare_reduce_fusion
  46.6 0.6 fusion.10
  47.2 1.6 custom-call.16
  48.8 0.2 fusion.13
  49.0 0.1 fusion.11
  49.2 5.0 %fusion = bf16[8192,128]{0,1:T(8,128)(2,1)S(1)} fusion(f32[21,128]{1,0:T(8,128)S(1)} %fusion.11, bf16[8192,128]{0,1:T(8,128)(2,1)} %copy.13, f32[20,8192]{1,0:T(8,128)S(1)} %copy-done.1), kind=kOutput, calls=%fused_computation.4 | convolution fusion | flops 267386880 | bytes 4860416 | tf_op jit(solution)/shard_map/dot_general | solution.py:18
  54.2 2.7 %collective-permute-start = (bf16[8192,128]{0,1:T(8,128)(2,1)S(1)}, bf16[8192,128]{0,1:T(8,128)(2,1)}, u32[]{:S(2)}, u32[]{:S(2)}) collective-permute-start(bf16[8192,128]{0,1:T(8,128)(2,1)S(1)} %fusion), channel_id=1, source_target_pairs={{0,4},{4,8},{8,12},{12,16},{16,20},{20,24},{24,28},{1,5},{5,9},{9,... | collective-permute-start | bytes 6291464 | tf_op jit(solution)/shard_map/ppermute | solution.py:13
  56.9 1.3 collective-permute-start.2
  58.2 1.3 collective-permute-done
  59.4 24.6 %collective-permute-start.1 = (bf16[8192,128]{0,1:T(8,128)(2,1)}, bf16[8192,128]{0,1:T(8,128)(2,1)}, u32[]{:S(2)}, u32[]{:S(2)}) collective-permute-start(bf16[8192,128]{0,1:T(8,128)(2,1)} %collective-permute-done), channel_id=1, source_target_pairs={{0,4},{4,8},{8,12},{12,16},{16,20},{20,24},{24,28},{1,5},{5,9},{9,... | collective-permute-start | bytes 6291464 | tf_op jit(solution)/shard_map/ppermute | solution.py:13
  84.7 0.0 copy-done.4
  84.7 0.1 pad_dynamic-slice_fusion.1
  84.8 0.7 fusion.43
  85.4 3.1 %fusion.37 = s32[640]{0:T(1024)S(1)} fusion(s32[]{:T(128)} %bitcast, s32[]{:T(128)} %bitcast.1, s32[]{:T(128)} %bitcast.2, s32[]{:T(128)} %bitcast.4, s32[]{:T(128)} %bitcast.3), kind=kLoop, calls=%fused_computation.68 | loop fusion | flops 12160 | bytes 2580 | tf_op jit(solution)/shard_map/gather | solution.py:65
  88.6 0.0 copy-done.2
  88.6 0.1 pad_dynamic-slice_fusion
  88.7 0.2 fusion.17
  88.9 0.2 fusion.15
  89.1 18.7 %multiply_reduce_fusion.1 = (f32[512]{0:T(512)S(1)}, bf16[8192,512]{1,0:T(8,128)(2,1)}) fusion(f32[21,512]{1,0:T(8,128)S(1)} %fusion.15, f32[20,8192]{1,0:T(8,128)S(1)} %copy-done.1, bf16[8192,512]{1,0:T(8,128)(2,1)} %param.7), kind=kOutput, calls=%fused_computation.1 | convolution fusion | flops 1082129920 | bytes 17477632 | tf_op jit(solution)/shard_map/dot_general | solution.py:18
  107.8 0.0 collective-permute-done.2
  107.8 1.5 collective-permute-start.3
  109.3 0.0 collective-permute-done.1
  109.3 1.7 constant_dynamic-update-slice_fusion.4
  111.0 1.7 constant_dynamic-update-slice_fusion.3
  112.8 0.2 constant_dynamic-update-slice_fusion.2
  112.9 1.7 constant_dynamic-update-slice_fusion.1
  114.7 0.1 collective-permute-done.3
  114.8 0.1 constant_dynamic-update-slice_fusion
  115.0 0.0 copy-start
  115.0 4.0 %copy-done = bf16[8192,640]{0,1:T(8,128)(2,1)} copy-done((bf16[8192,640]{0,1:T(8,128)(2,1)}, bf16[8192,640]{0,1:T(8,128)(2,1)S(1)}, u32[]{:S(2)}) %copy-start) | copy-done | bytes 10485784
  119.0 10.0 %fusion.44 = f32[512,640]{1,0:T(8,128)} fusion(bf16[8192,512]{1,0:T(8,128)(2,1)} %get-tuple-element.16, bf16[8192,640]{0,1:T(8,128)(2,1)S(1)} %constant_dynamic-update-slice_fusion), kind=kOutput, calls=%fused_computation.78 | convolution fusion | flops 5368709120 | bytes 20185088 | tf_op jit(solution)/shard_map/dot_general | solution.py:23
  129.0 0.0 copy-start.3
  129.0 0.0 all-reduce.7.cloned.1.call-update
  129.0 6.1 %multiply_reduce_fusion = f32[640]{0:T(1024)S(1)} fusion(bf16[8192,640]{0,1:T(8,128)(2,1)} %copy-done), kind=kLoop, calls=%fused_computation | loop fusion | flops 15728000 | bytes 10488320 | tf_op jit(solution)/shard_map/reduce_sum | solution.py:52
  135.1 8.5 %all-reduce.3 = (f32[640]{0:T(1024)S(1)}, f32[512]{0:T(512)S(1)}) all-reduce(f32[640]{0:T(1024)S(1)} %multiply_reduce_fusion, f32[512]{0:T(512)S(1)} %get-tuple-element.15), channel_id=1, replica_groups=mesh['genome'=8,'sample'=4] {'sample'}, use_global_device_ids=true, to_apply=%region_9.10 | all-reduce | flops 1152 | bytes 9216 | tf_op jit(solution)/shard_map/psum | solution.py:52
  143.6 0.1 add_sqrt_fusion.1
  143.7 85.9 %all-reduce.7.cloned.1.call-done = f32[512,640]{1,0:T(8,128)} async-done(((f32[512,640]{1,0:T(8,128)}), f32[512,640]{1,0:T(8,128)}) %all-reduce.7.cloned.1.call-update) | async-done | bytes 1310736 | tf_op jit(solution)/shard_map/psum | solution.py:55
  229.6 0.0 copy-done.3
  229.6 1.9 divide_select_fusion
  (4 shorter events, 0.1 us)
Async XLA Ops:
  6.5 9.4 %copy-start.1 = (f32[20,8192]{1,0:T(8,128)S(1)}, f32[20,8192]{1,0:T(8,128)}, u32[]{:S(2)}) copy-start(f32[20,8192]{1,0:T(8,128)} %param.9) | copy-start | bytes 1966084
  6.5 223.1 %all-reduce.7.cloned.1.call-start = ((), (), s32[]{:S(2)}) async-start(), calls=%async_computation | async-start | bytes 2621440 | tf_op jit(solution)/shard_map/psum | solution.py:55
  11.8 72.9 %copy-start.4 = (s32[8]{0:T(128)S(1)}, s32[8]{0:T(128)}, u32[]{:S(2)}) copy-start(s32[8]{0:T(128)} %param.11) | copy-start | bytes 100
  11.8 76.8 %copy-start.2 = (s32[1024]{0:T(1024)S(1)}, s32[1024]{0:T(1024)}, u32[]{:S(2)}) copy-start(s32[1024]{0:T(1024)} %param.10) | copy-start | bytes 12292
  54.2 5.2 %collective-permute-start = (bf16[8192,128]{0,1:T(8,128)(2,1)S(1)}, bf16[8192,128]{0,1:T(8,128)(2,1)}, u32[]{:S(2)}, u32[]{:S(2)}) collective-permute-start(bf16[8192,128]{0,1:T(8,128)(2,1)S(1)} %fusion), channel_id=1, source_target_pairs={{0,4},{4,8},{8,12},{12,16},{16,20},{20,24},{24,28},{1,5},{5,9},{9,... | collective-permute-start | bytes 6291464 | tf_op jit(solution)/shard_map/ppermute | solution.py:13
  56.9 50.9 %collective-permute-start.2 = (bf16[8192,128]{0,1:T(8,128)(2,1)S(1)}, bf16[8192,128]{0,1:T(8,128)(2,1)}, u32[]{:S(2)}, u32[]{:S(2)}) collective-permute-start(bf16[8192,128]{0,1:T(8,128)(2,1)S(1)} %fusion), channel_id=1, source_target_pairs={{4,0},{8,4},{12,8},{16,12},{20,16},{24,20},{28,24},{5,1},{9,5},{13... | collective-permute-start | bytes 6291464 | tf_op jit(solution)/shard_map/ppermute | solution.py:13
  59.4 49.9 %collective-permute-start.1 = (bf16[8192,128]{0,1:T(8,128)(2,1)}, bf16[8192,128]{0,1:T(8,128)(2,1)}, u32[]{:S(2)}, u32[]{:S(2)}) collective-permute-start(bf16[8192,128]{0,1:T(8,128)(2,1)} %collective-permute-done), channel_id=1, source_target_pairs={{0,4},{4,8},{8,12},{12,16},{16,20},{20,24},{24,28},{1,5},{5,9},{9,... | collective-permute-start | bytes 6291464 | tf_op jit(solution)/shard_map/ppermute | solution.py:13
  107.8 7.0 %collective-permute-start.3 = (bf16[8192,128]{0,1:T(8,128)(2,1)}, bf16[8192,128]{0,1:T(8,128)(2,1)S(1)}, u32[]{:S(2)}, u32[]{:S(2)}) collective-permute-start(bf16[8192,128]{0,1:T(8,128)(2,1)} %collective-permute-done.2), channel_id=1, source_target_pairs={{4,0},{8,4},{12,8},{16,12},{20,16},{24,20},{28,24},{5,1},{9,5},{13... | collective-permute-start | bytes 6291464 | tf_op jit(solution)/shard_map/ppermute | solution.py:13
  115.0 4.0 %copy-start = (bf16[8192,640]{0,1:T(8,128)(2,1)}, bf16[8192,640]{0,1:T(8,128)(2,1)S(1)}, u32[]{:S(2)}) copy-start(bf16[8192,640]{0,1:T(8,128)(2,1)S(1)} %constant_dynamic-update-slice_fusion) | copy-start | bytes 31457284
  129.0 100.7 %copy-start.3 = (s32[128]{0:T(128)S(1)}, s32[128]{0:T(128)}, u32[]{:S(2)}) copy-start(s32[128]{0:T(128)} %param.13) | copy-start | bytes 1540
Sparse Core Ops, SparseCore 0:
  129.1 100.4 all-reduce.6
where the time goes:
time: 239 us; the launch traced here: 238 us
  waiting for transfers between devices  87.3 us (37%)
  matrix products  45.6 us (19%)
  blocking collectives  30.5 us (13%)
  starting transfers between devices  30 us (13%)
  other arithmetic  16.1 us (7%)
  local copies, waits for them, and re-layouts  14.5 us (6%)
  between operations  14.2 us (6%)
    psum x1, waiting for transfers between devices, local(): total = lax.psum(variant_products(geno_res, window), 'sample')  85.9 us
    ppermute x4, starting transfers between devices, from_behind(): lax.ppermute(value, axis, [(source, source + steps) for source in range(f...  30 us
    dot_general x2, matrix products, fitted_part(): fitted = jnp.dot(basis.T, coef, precision=lax.Precision.HIGHEST)  23.7 us
    psum x1, blocking collectives, local(): lax.psum((gram, cross_geno, cross_probe), 'sample')  22 us
    unnamed x15, local copies, waits for them, and re-layouts  13.5 us
    dot_general x1, matrix products, variant_products(): lax.dot_general(left, right, (((0,), (0,)), ((), ())), preferred_element_...  10 us
    psum x1, blocking collectives, local(): lax.psum((jnp.sum(gres32 * gres32, 0), jnp.sum(win32 * win32, 0)), 'sample')  8.5 us
    reduce_sum x1, other arithmetic, local(): jnp.sum(win32 * win32, 0)  6.1 us
  transfers between devices with their start and end apart: 5, of which 3 were waited for; matrix products, arithmetic and copies ran while one was open for 15% of the time, Pallas kernels for 0%

commit v1 on v0

--- a/solution.py
+++ b/solution.py
@@ -1,6 +1,10 @@
+import functools
+
 import jax
 import jax.numpy as jnp
 from jax import lax
+from jax.experimental import pallas as pl
+from jax.experimental.pallas import tpu as pltpu
 from jax.sharding import PartitionSpec as P
 
 REACH = 2
@@ -74,6 +78,343 @@
     return jnp.where(tested, value, jnp.float32(0.0))
 
 
+F32 = jnp.float32
+BF16 = jnp.bfloat16
+MESH = pl.DeviceIdType.MESH
+HIGH = lax.Precision.HIGHEST
+PARTS = 8
+
+
+def split3(value):
+    hi = value.astype(BF16)
+    rest = value - hi.astype(F32)
+    mid = rest.astype(BF16)
+    lo = (rest - mid.astype(F32)).astype(BF16)
+    return hi, mid, lo
+
+
+def scan_kernel(
+    ncov, scale, geno_hbm, probe_hbm, cov_ref, out_ref,
+    geno, probe, basis, base, stack, geno_t, around, sib_own, sib_next, acc, gathered,
+    share, coef6, coefp, bgr, infos, pnorms, pnorms_in, acc_in,
+    load_sem, x_send, x_recv, y_send, y_recv, c_send, c_recv, o_send, o_recv,
+    g_send, g_recv, m_send, m_recv, n_send, n_recv, z_send, z_recv,
+):
+    rows, width_v = geno.shape
+    width_p = probe.shape[1]
+    part = rows // PARTS
+    ncol = width_v + width_p
+    g = lax.axis_index("genome")
+    z = lax.axis_index("sample")
+    core = g % 2
+    x = (g // 2) % 2
+    sib = g + 1 - 2 * core
+    beside = g + 2 - 4 * x
+    above = g + 4 - 8 * (g // 4)
+    same = core * x + (1 - core) * (1 - x)
+    onward = 1 - same
+
+    def remote(src, dst, send, recv, **where):
+        return pltpu.make_async_remote_copy(
+            src_ref=src, dst_ref=dst, send_sem=send, recv_sem=recv,
+            device_id=dict(where), device_id_type=MESH,
+        )
+
+    def sl(k):
+        return pl.ds(pl.multiple_of(k * part, part), part)
+
+    def x_copy(k):
+        return remote(probe_hbm.at[sl(k)], around.at[0, sl(k)], x_send.at[k], x_recv.at[k], genome=beside)
+
+    def y_copy(k):
+        return remote(around.at[0, sl(k)], around.at[1, sl(k)], y_send.at[k], y_recv.at[k], genome=above)
+
+    def c_copy(k):
+        return remote(around.at[onward, sl(k)], sib_next.at[sl(k)], c_send.at[k], c_recv.at[k], genome=sib)
+
+    own_copy = remote(probe_hbm, sib_own, o_send, o_recv, genome=sib)
+    load_p = pltpu.make_async_copy(probe_hbm, probe, load_sem.at[0])
+    load_g = pltpu.make_async_copy(geno_hbm, geno, load_sem.at[1])
+
+    def peer(d):
+        return (z + d) % 4
+
+    def g_copy(d):
+        return remote(share, gathered.at[d - 1], g_send.at[d - 1], g_recv.at[d - 1], sample=peer(d))
+
+    def m_copy(n, d):
+        return remote(infos.at[2], infos.at[2 - d], m_send.at[n], m_recv.at[n], genome=(g + d + 8) % 8)
+
+    def n_copy(d):
+        return remote(pnorms, pnorms_in.at[d - 1], n_send.at[d - 1], n_recv.at[d - 1], sample=peer(d))
+
+    def z_copy(t, d):
+        mine = pl.ds(pl.multiple_of(peer(d) * 128, 128), 128)
+        return remote(acc.at[t, mine], acc_in.at[d - 1, t], z_send.at[t, d - 1], z_recv.at[t, d - 1], sample=peer(d))
+
+    load_p.start()
+    load_g.start()
+    barrier = pltpu.get_barrier_semaphore()
+    near = [sib, beside, above] + [(g + d + 8) % 8 for d in (1, 2, -1, -2)]
+    for other in near:
+        pl.semaphore_signal(barrier, inc=1, device_id={"genome": other}, device_id_type=MESH)
+    for d in (1, 2, 3):
+        pl.semaphore_signal(barrier, inc=1, device_id={"sample": peer(d)}, device_id_type=MESH)
+    pl.semaphore_wait(barrier, len(near) + 3)
+
+    @pl.loop(0, PARTS)
+    def _(k):
+        x_copy(k).start()
+
+    own_copy.start()
+
+    basis[...] = jnp.zeros_like(basis)
+    base[...] = jnp.zeros_like(base)
+    share[...] = jnp.zeros_like(share)
+    acc[...] = jnp.zeros_like(acc)
+    bgr[...] = jnp.zeros_like(bgr)
+    load_p.wait()
+    load_g.wait()
+
+    @pl.loop(0, PARTS)
+    def _(k):
+        basis[0:ncov, :] = cov_ref[:, sl(k)]
+        basis[ncov : ncov + 1, :] = jnp.ones((1, part), F32)
+        b = basis[...]
+        hi, mid, lo = split3(b)
+        for n, piece in enumerate((hi, hi, mid, hi, mid, lo)):
+            stack[k, 32 * n : 32 * n + 32, :] = piece
+        b3 = stack[k, 96:192, :]
+        both = ((geno, 0, width_v), (probe, width_v, width_p))
+        for ref, first, width in both:
+            got = jnp.dot(b3, ref[sl(k), :], preferred_element_type=F32)
+            share[:, first : first + width] += got[0:32] + got[32:64] + got[64:96]
+        base[0:32, :] = b
+        share[:, ncol : ncol + 128] += lax.dot_general(
+            b, base[...], (((1,), (1,)), ((), ())), precision=HIGH, preferred_element_type=F32
+        )
+
+    for d in (1, 2, 3):
+        g_copy(d).start()
+    x_copy(0).wait_recv()
+    y_copy(0).start()
+    for d in (1, 2, 3):
+        g_copy(d).wait_recv()
+    lane = lax.broadcasted_iota(jnp.int32, (32, 128), 1)
+    line = lax.broadcasted_iota(jnp.int32, (32, ncol + 128), 0)
+
+    def eliminate(k, a):
+        col = jnp.sum(jnp.where(lane == k, a[:, ncol:], 0.0), axis=1, keepdims=True)
+        row = jnp.sum(jnp.where(line == k, a, 0.0), axis=0, keepdims=True)
+        pivot = jnp.sum(jnp.where(lane[0:1] == k, row[:, ncol:], 0.0), axis=1, keepdims=True)
+        row = row / pivot
+        return jnp.where(line == k, row, a - col * row)
+
+    solved = lax.fori_loop(
+        0, ncov + 1, eliminate, share[...] + gathered[0] + gathered[1] + gathered[2]
+    )
+    hi, mid, lo = split3(solved[:, 0:ncol])
+    for n, piece in enumerate((hi, mid, hi, lo, mid, hi)):
+        coef6[32 * n : 32 * n + 32, :] = piece
+    infos[2] = solved[:, width_v:ncol]
+
+    @pl.loop(0, PARTS)
+    def _(k):
+        fit = lax.dot_general(
+            stack[k], coef6[:, width_v:ncol], (((0,), (0,)), ((), ())), preferred_element_type=F32
+        )
+        res = (probe[sl(k), :].astype(F32) - fit).astype(BF16).astype(F32)
+        infos[2, 24:25, :] += jnp.sum(res * res, axis=0, keepdims=True)
+
+    for n, d in enumerate((1, 2, -1, -2)):
+        m_copy(n, d).start()
+    x_copy(1).wait_recv()
+    y_copy(1).start()
+
+    def residual(k):
+        fit = lax.dot_general(
+            coef6[:, 0:width_v], stack[k], (((0,), (0,)), ((), ())), preferred_element_type=F32
+        )
+        res = (jnp.transpose(geno[sl(k), :]).astype(F32) - fit).astype(BF16)
+        geno_t[k] = res
+        bgr[...] += lax.dot_general(
+            res, stack[k, 96:192, :], (((1,), (1,)), ((), ())), preferred_element_type=F32
+        )
+        acc[0] += jnp.dot(res, probe[sl(k), :], preferred_element_type=F32)
+        wide = res.astype(F32)
+        wide = wide * wide
+        total = wide[:, 0:128]
+        for n in range(1, part // 128):
+            total = total + wide[:, 128 * n : 128 * n + 128]
+        acc[5] += total
+
+    @pl.loop(0, PARTS // 2)
+    def _(i):
+        residual(2 * i)
+        residual(2 * i + 1)
+        x_copy(i + 2).wait_recv()
+        y_copy(i + 2).start()
+
+    for n, d in enumerate((1, 2, -1, -2)):
+        m_copy(n, d).wait_recv()
+    for j in range(5):
+        pnorms[j] = jnp.broadcast_to(infos[j, 24:25, :], (8, 128))
+    for d in (1, 2, 3):
+        n_copy(d).start()
+
+    places = (2, 3 - 2 * core, 4 - 4 * x, 4 * x, 1 + 2 * core)
+
+    def correct(t):
+        for n in range(3):
+            coefp[32 * n : 32 * n + 32, :] = infos[places[t]]
+        acc[t] = acc[t] - jnp.dot(
+            bgr[...], coefp[...], precision=HIGH, preferred_element_type=F32
+        )
+
+    own_copy.wait_recv()
+
+    @pl.loop(0, PARTS)
+    def _(k):
+        acc[1] += jnp.dot(geno_t[k], sib_own[sl(k), :], preferred_element_type=F32)
+
+    for t in range(5):
+        correct(t)
+    for t in (0, 1, 5):
+        for d in (1, 2, 3):
+            z_copy(t, d).start()
+
+    def arrive(k):
+        y_copy(k).wait_recv()
+        c_copy(k).start()
+        acc[2] += jnp.dot(geno_t[k], around[0, sl(k), :], preferred_element_type=F32)
+        acc[3] += jnp.dot(geno_t[k], around[1, sl(k), :], preferred_element_type=F32)
+
+    def beside_next(k):
+        c_copy(k).wait_recv()
+        acc[4] += jnp.dot(geno_t[k], sib_next[sl(k), :], preferred_element_type=F32)
+
+    for k in (6, 7):
+        arrive(k - 6)
+        x_copy(k).wait_recv()
+        y_copy(k).start()
+    beside_next(0)
+
+    @pl.loop(2, PARTS)
+    def _(k):
+        arrive(k)
+        beside_next(k - 1)
+
+    for t in (2, 3):
+        for d in (1, 2, 3):
+            z_copy(t, d).start()
+    beside_next(PARTS - 1)
+    for d in (1, 2, 3):
+        z_copy(4, d).start()
+
+    for d in (1, 2, 3):
+        n_copy(d).wait_recv()
+    mine = pl.ds(pl.multiple_of(z * 128, 128), 128)
+
+    def total(t):
+        for d in (1, 2, 3):
+            z_copy(t, d).wait_recv()
+        return acc[t, mine] + acc_in[0, t] + acc_in[1, t] + acc_in[2, t]
+
+    gnorm = jnp.sqrt(jnp.sum(total(5), axis=1, keepdims=True) + 1e-06)
+    for t in range(5):
+        j = places[t]
+        pn = pnorms[j] + pnorms_in[0, j] + pnorms_in[1, j] + pnorms_in[2, j]
+        pn = jnp.sqrt(pn[0:1] + 1e-06)
+        out_ref[:, pl.ds(pl.multiple_of(j * 128, 128), 128)] = scale * total(t) / (gnorm * pn)
+
+    own_copy.wait_send()
+    for n, d in enumerate((1, 2, -1, -2)):
+        m_copy(n, d).wait_send()
+    for d in (1, 2, 3):
+        g_copy(d).wait_send()
+        n_copy(d).wait_send()
+        for t in range(6):
+            z_copy(t, d).wait_send()
+
+    @pl.loop(0, PARTS)
+    def _(k):
+        x_copy(k).wait_send()
+        y_copy(k).wait_send()
+        c_copy(k).wait_send()
+
+
+def scan(genotypes, probes, covariates, total_rows):
+    rows, width_v = genotypes.shape
+    width_p = probes.shape[1]
+    ncov = covariates.shape[0]
+    part = rows // PARTS
+    ncol = width_v + width_p
+    dma = pltpu.SemaphoreType.DMA
+    scale = float(total_rows - ncov - 2) ** 0.5
+    block = jax.ShapeDtypeStruct((128, 5 * width_p), F32)
+
+    scratch = [
+        pltpu.VMEM((rows, width_v), BF16),
+        pltpu.VMEM((rows, width_p), BF16),
+        pltpu.VMEM((32, part), F32),
+        pltpu.VMEM((128, part), F32),
+        pltpu.VMEM((PARTS, 192, part), BF16),
+        pltpu.VMEM((PARTS, width_v, part), BF16),
+        pltpu.VMEM((2, rows, width_p), BF16),
+        pltpu.VMEM((rows, width_p), BF16),
+        pltpu.VMEM((rows, width_p), BF16),
+        pltpu.VMEM((6, width_v, 128), F32),
+        pltpu.VMEM((3, 32, ncol + 128), F32),
+        pltpu.VMEM((32, ncol + 128), F32),
+        pltpu.VMEM((192, ncol), BF16),
+        pltpu.VMEM((96, 128), F32),
+        pltpu.VMEM((width_v, 96), F32),
+        pltpu.VMEM((5, 32, 128), F32),
+        pltpu.VMEM((5, 8, 128), F32),
+        pltpu.VMEM((3, 5, 8, 128), F32),
+        pltpu.VMEM((3, 6, 128, 128), F32),
+        dma((2,)),
+        dma((PARTS,)), dma((PARTS,)), dma((PARTS,)), dma((PARTS,)), dma((PARTS,)), dma((PARTS,)),
+        dma, dma,
+        dma((3,)), dma((3,)), dma((4,)), dma((4,)), dma((3,)), dma((3,)), dma((6, 3)), dma((6, 3)),
+    ]
+    return pl.pallas_call(
+        functools.partial(scan_kernel, ncov, scale),
+        out_shape=block,
+        in_specs=[
+            pl.BlockSpec(memory_space=pl.ANY),
+            pl.BlockSpec(memory_space=pl.ANY),
+            pl.BlockSpec(memory_space=pltpu.VMEM),
+        ],
+        out_specs=pl.BlockSpec(memory_space=pltpu.VMEM),
+        scratch_shapes=scratch,
+        cost_estimate=pl.CostEstimate(flops=8 * 10**9, bytes_accessed=12 * 10**6, transcendentals=0),
+        compiler_params=pltpu.CompilerParams(
+            collective_id=0, has_side_effects=True, vmem_limit_bytes=56 * 2**20
+        ),
+    )(genotypes, probes, covariates)
+
+
+def fused(genotypes, probes, covariates, probe_locus, probe_counts, reach, positions):
+    width_p = probes.shape[1]
+    nblk = probe_counts.shape[0]
+    wide = (2 * REACH + 1) * width_p
+    samples = genotypes.shape[0] * lax.axis_size("sample")
+    value = scan(genotypes, probes, covariates, samples)
+    block = lax.axis_index("genome")
+    column = jnp.arange(wide, dtype=jnp.int32)
+    offset_of = column // width_p - REACH
+    slot_of = column % width_p
+    padded_start = jnp.pad(probe_locus, (REACH * width_p, REACH * width_p))
+    padded_count = jnp.pad(probe_counts, (REACH, REACH))
+    starts = lax.dynamic_slice_in_dim(padded_start, block * width_p, wide, 0)
+    counted = lax.dynamic_slice_in_dim(padded_count, block, 2 * REACH + 1, 0)[column // width_p]
+    inside = (block + offset_of >= 0) & (block + offset_of < nblk)
+    tested = inside & (slot_of < counted) & (jnp.abs(offset_of) <= reach[0])
+    tested = tested[None, :] & (jnp.abs(positions[:, None] - starts[None, :]) <= WIN)
+    return jnp.where(tested, value, jnp.float32(0.0))
+
+
 def solution(mesh):
     placed = (
         P("sample", "genome"),
@@ -84,6 +425,7 @@
         P("genome"),
         P(("genome", "sample")),
     )
+    sizes = (mesh.shape["genome"], mesh.shape["sample"])
     return jax.shard_map(
-        local, mesh=mesh, in_specs=placed, out_specs=P(("genome", "sample"), None), check_vma=False
+        fused if sizes == (8, 4) else local, mesh=mesh, in_specs=placed, out_specs=P(("genome", "sample"), None), check_vma=False
     )

time: 239 us -> 104 us (0.44)
  Pallas kernels: 0 us -> 95.8 us
  waiting for transfers between devices: 87.3 us -> 0 us
  matrix products: 45.6 us -> 0 us
  blocking collectives: 30.5 us -> 0 us
  starting transfers between devices: 30 us -> 0 us
  between operations: 14.2 us -> 0.68 us
  local copies, waits for them, and re-layouts: 14.5 us -> 2.18 us
  other arithmetic: 16.1 us -> 4.96 us
    pallas_call x0 -> x1, Pallas kernels: none -> 95.8 us  [scan(): pl.pallas_call(functools.partial(scan_kernel, ncov, scale), out_shape=blo...]
    psum x1 -> x0, waiting for transfers between devices: 85.9 us -> none  [local(): total = lax.psum(variant_products(geno_res, window), 'sample')]
    dot_general x6 -> x0, matrix products: 44.9 us -> none  [the longest x2 23.7 us: fitted_part(): fitted = jnp.dot(basis.T, coef, precision=lax.Precision.HIGHEST)]
    psum x2 -> x0, blocking collectives: 30.5 us -> none  [the longest x1 22 us: local(): lax.psum((gram, cross_geno, cross_probe), 'sample')]
    ppermute x4 -> x0, starting transfers between devices: 30 us -> none  [from_behind(): lax.ppermute(value, axis, [(source, source + steps) for source in range(f...]
    unnamed x15 -> x2, local copies, waits for them, and re-layouts: 13.5 us -> 0.01 us
    reduce_sum x1 -> x0, other arithmetic: 6.1 us -> none  [local(): jnp.sum(win32 * win32, 0)]
    another operation x5 -> x0, other arithmetic: 4.84 us -> none  [the longest x3 2.58 us: local(): factor = jnp.linalg.cholesky(gram)]
  transfers between devices with their start and end apart: 5 -> 0, of which waited for: 3 -> 0; matrix products, arithmetic and copies ran while one was open for 15% -> 0% of each run, Pallas kernels for 0% -> 0%
where the time goes in v1:
time: 104 us
  Pallas kernels  95.8 us (92%)
  other arithmetic  4.96 us (5%)
  local copies, waits for them, and re-layouts  2.18 us (2%)
    pallas_call x1, Pallas kernels, scan(): pl.pallas_call(functools.partial(scan_kernel, ncov, scale), out_shape=blo...  95.8 us
    gather x1, other arithmetic, fused(): lax.dynamic_slice_in_dim(padded_count, block, 2 * REACH + 1, 0)  3.09 us

profile of v1, /device:TPU:0, one launch (start us, length us, event | category | flops | bytes accessed | tf_op | source)
XLA Modules:
  0.0 103.6 jit_solution(6976556093642760759)
XLA Ops:
  0.7 0.7 pad_dynamic-slice_fusion.1
  1.4 0.7 fusion.20
  2.1 3.1 %fusion.19 = s32[640]{0:T(1024)S(1)} fusion(s32[]{:T(128)} %bitcast, s32[]{:T(128)} %bitcast.1, s32[]{:T(128)} %bitcast.2, s32[]{:T(128)} %bitcast.4, s32[]{:T(128)} %bitcast.3), kind=kLoop, calls=%fused_computation.34 | loop fusion | flops 12160 | bytes 2580 | tf_op jit(solution)/shard_map/gather | solution.py:411
  5.2 0.8 pad_dynamic-slice_fusion
  5.9 0.0 copy-start
  5.9 95.8 %shard_map.73 = f32[128,640]{1,0:T(8,128)} custom-call(bf16[8192,512]{1,0:T(8,128)(2,1)} %geno_hbm.1, bf16[8192,128]{1,0:T(8,128)(2,1)} %probe_hbm.1, f32[20,8192]{1,0:T(8,128)} %cov_ref.1), custom_call_target="tpu_custom_call" | custom-call | flops 8000000000 | bytes 12000000 | tf_op jit(solution)/shard_map/pallas_call | solution.py:381
  101.8 0.0 copy-done
  101.8 1.9 %fusion.1 = f32[128,640]{1,0:T(8,128)} fusion(f32[128,640]{1,0:T(8,128)} %shard_map.73, s32[640]{0:T(1024)S(1)} %pad_dynamic-slice_fusion, s32[128]{0:T(128)S(1)} %copy-done, pred[640]{0:T(1024)(128)(4,1)S(1)} %fusion.16), kind=kLoop, calls=%fused_computation.2 | loop fusion | flops 409600 | bytes 659072 | tf_op jit(solution)/shard_map/jit(_where)/select_n | solution.py:415
  (1 shorter events, 0.0 us)
Async XLA Ops:
  5.9 95.8 %copy-start = (s32[128]{0:T(128)S(1)}, s32[128]{0:T(128)}, u32[]{:S(2)}) copy-start(s32[128]{0:T(128)} %param.13) | copy-start | bytes 1540

commit v2 on v1

--- a/solution.py
+++ b/solution.py
@@ -96,7 +96,7 @@
 def scan_kernel(
     ncov, scale, geno_hbm, probe_hbm, cov_ref, out_ref,
     geno, probe, basis, base, stack, geno_t, around, sib_own, sib_next, acc, gathered,
-    share, coef6, coefp, bgr, infos, pnorms, pnorms_in, acc_in,
+    share, coef6, coefp, bgr, infos, pnorms, pnorms_in, acc_in, late, late_in,
     load_sem, x_send, x_recv, y_send, y_recv, c_send, c_recv, o_send, o_recv,
     g_send, g_recv, m_send, m_recv, n_send, n_recv, z_send, z_recv,
 ):
@@ -150,6 +150,11 @@
 
     def z_copy(t, d):
         mine = pl.ds(pl.multiple_of(peer(d) * 128, 128), 128)
+        if 2 <= t <= 4:
+            return remote(
+                late.at[t - 2, mine], late_in.at[d - 1, t - 2],
+                z_send.at[t, d - 1], z_recv.at[t, d - 1], sample=peer(d),
+            )
         return remote(acc.at[t, mine], acc_in.at[d - 1, t], z_send.at[t, d - 1], z_recv.at[t, d - 1], sample=peer(d))
 
     load_p.start()
@@ -167,6 +172,10 @@
         x_copy(k).start()
 
     own_copy.start()
+
+    def onto(k):
+        x_copy(k).wait_recv()
+        y_copy(k).start()
 
     basis[...] = jnp.zeros_like(basis)
     base[...] = jnp.zeros_like(base)
@@ -176,8 +185,7 @@
     load_p.wait()
     load_g.wait()
 
-    @pl.loop(0, PARTS)
-    def _(k):
+    def crossed(k):
         basis[0:ncov, :] = cov_ref[:, sl(k)]
         basis[ncov : ncov + 1, :] = jnp.ones((1, part), F32)
         b = basis[...]
@@ -194,10 +202,12 @@
             b, base[...], (((1,), (1,)), ((), ())), precision=HIGH, preferred_element_type=F32
         )
 
+    pl.loop(0, PARTS - 2)(crossed)
+    onto(0)
+    pl.loop(PARTS - 2, PARTS)(crossed)
     for d in (1, 2, 3):
         g_copy(d).start()
-    x_copy(0).wait_recv()
-    y_copy(0).start()
+    onto(1)
     for d in (1, 2, 3):
         g_copy(d).wait_recv()
     lane = lax.broadcasted_iota(jnp.int32, (32, 128), 1)
@@ -210,9 +220,12 @@
         row = row / pivot
         return jnp.where(line == k, row, a - col * row)
 
-    solved = lax.fori_loop(
-        0, ncov + 1, eliminate, share[...] + gathered[0] + gathered[1] + gathered[2]
-    )
+    solved = share[...] + gathered[0] + gathered[1] + gathered[2]
+    half = (ncov + 1) // 2
+    solved = lax.fori_loop(0, half, eliminate, solved)
+    onto(2)
+    solved = lax.fori_loop(half, ncov + 1, eliminate, solved)
+    onto(3)
     hi, mid, lo = split3(solved[:, 0:ncol])
     for n, piece in enumerate((hi, mid, hi, lo, mid, hi)):
         coef6[32 * n : 32 * n + 32, :] = piece
@@ -228,8 +241,7 @@
 
     for n, d in enumerate((1, 2, -1, -2)):
         m_copy(n, d).start()
-    x_copy(1).wait_recv()
-    y_copy(1).start()
+    onto(4)
 
     def residual(k):
         fit = lax.dot_general(
@@ -248,12 +260,10 @@
             total = total + wide[:, 128 * n : 128 * n + 128]
         acc[5] += total
 
-    @pl.loop(0, PARTS // 2)
-    def _(i):
-        residual(2 * i)
-        residual(2 * i + 1)
-        x_copy(i + 2).wait_recv()
-        y_copy(i + 2).start()
+    pl.loop(0, PARTS // 2)(residual)
+    onto(5)
+    pl.loop(PARTS // 2, PARTS)(residual)
+    onto(6)
 
     for n, d in enumerate((1, 2, -1, -2)):
         m_copy(n, d).wait_recv()
@@ -293,21 +303,20 @@
         c_copy(k).wait_recv()
         acc[4] += jnp.dot(geno_t[k], sib_next[sl(k), :], preferred_element_type=F32)
 
-    for k in (6, 7):
-        arrive(k - 6)
-        x_copy(k).wait_recv()
-        y_copy(k).start()
-    beside_next(0)
-
-    @pl.loop(2, PARTS)
+    arrive(0)
+    onto(7)
+
+    @pl.loop(1, PARTS)
     def _(k):
         arrive(k)
         beside_next(k - 1)
 
     for t in (2, 3):
+        late[t - 2] = acc[t].astype(BF16)
         for d in (1, 2, 3):
             z_copy(t, d).start()
     beside_next(PARTS - 1)
+    late[2] = acc[4].astype(BF16)
     for d in (1, 2, 3):
         z_copy(4, d).start()
 
@@ -318,6 +327,9 @@
     def total(t):
         for d in (1, 2, 3):
             z_copy(t, d).wait_recv()
+        if 2 <= t <= 4:
+            got = [late_in[n, t - 2].astype(F32) for n in range(3)]
+            return acc[t, mine] + got[0] + got[1] + got[2]
         return acc[t, mine] + acc_in[0, t] + acc_in[1, t] + acc_in[2, t]
 
     gnorm = jnp.sqrt(jnp.sum(total(5), axis=1, keepdims=True) + 1e-06)
@@ -373,6 +385,8 @@
         pltpu.VMEM((5, 8, 128), F32),
         pltpu.VMEM((3, 5, 8, 128), F32),
         pltpu.VMEM((3, 6, 128, 128), F32),
+        pltpu.VMEM((3, width_v, 128), BF16),
+        pltpu.VMEM((3, 3, 128, 128), BF16),
         dma((2,)),
         dma((PARTS,)), dma((PARTS,)), dma((PARTS,)), dma((PARTS,)), dma((PARTS,)), dma((PARTS,)),
         dma, dma,
@@ -402,16 +416,16 @@
     samples = genotypes.shape[0] * lax.axis_size("sample")
     value = scan(genotypes, probes, covariates, samples)
     block = lax.axis_index("genome")
-    column = jnp.arange(wide, dtype=jnp.int32)
-    offset_of = column // width_p - REACH
-    slot_of = column % width_p
+    offset = jnp.arange(-REACH, REACH + 1, dtype=jnp.int32)[:, None]
+    slot = jnp.arange(width_p, dtype=jnp.int32)[None, :]
     padded_start = jnp.pad(probe_locus, (REACH * width_p, REACH * width_p))
     padded_count = jnp.pad(probe_counts, (REACH, REACH))
     starts = lax.dynamic_slice_in_dim(padded_start, block * width_p, wide, 0)
-    counted = lax.dynamic_slice_in_dim(padded_count, block, 2 * REACH + 1, 0)[column // width_p]
-    inside = (block + offset_of >= 0) & (block + offset_of < nblk)
-    tested = inside & (slot_of < counted) & (jnp.abs(offset_of) <= reach[0])
-    tested = tested[None, :] & (jnp.abs(positions[:, None] - starts[None, :]) <= WIN)
+    counted = lax.dynamic_slice_in_dim(padded_count, block, 2 * REACH + 1, 0)[:, None]
+    inside = (block + offset >= 0) & (block + offset < nblk)
+    valid = inside & (slot < counted) & (jnp.abs(offset) <= reach[0])
+    limit = jnp.where(valid, WIN, -1).reshape(wide)
+    tested = jnp.abs(positions[:, None] - starts[None, :]) <= limit[None, :]
     return jnp.where(tested, value, jnp.float32(0.0))
 
 

time: 104 us -> 92 us (0.88)
  Pallas kernels: 95.8 us -> 87.7 us
  other arithmetic: 4.96 us -> 1.92 us
    pallas_call x1, Pallas kernels: 95.8 us -> 87.7 us  [scan(): pl.pallas_call(functools.partial(scan_kernel, ncov, scale), out_shape=blo...]
    gather x1 -> x0, other arithmetic: 3.09 us -> none  [fused(): lax.dynamic_slice_in_dim(padded_count, block, 2 * REACH + 1, 0)]
where the time goes in v2:
time: 92 us; the launch traced here: 91.8 us
  Pallas kernels  87.7 us (95%)
  other arithmetic  1.92 us (2%)
  local copies, waits for them, and re-layouts  1.51 us (2%)
    pallas_call x1, Pallas kernels, scan(): pl.pallas_call(functools.partial(scan_kernel, ncov, scale), out_shape=blo...  87.7 us

profile of v2, /device:TPU:0, one launch (start us, length us, event | category | flops | bytes accessed | tf_op | source)
XLA Modules:
  0.0 91.8 jit_solution(3650889612928226853)
XLA Ops:
  0.7 0.7 pad_dynamic-slice_fusion.1
  1.4 0.1 select_bitcast_fusion
  1.5 0.8 pad_dynamic-slice_fusion
  2.2 0.0 copy-start
  2.2 87.7 %shard_map.73 = f32[128,640]{1,0:T(8,128)} custom-call(bf16[8192,512]{1,0:T(8,128)(2,1)} %geno_hbm.1, bf16[8192,128]{1,0:T(8,128)(2,1)} %probe_hbm.1, f32[20,8192]{1,0:T(8,128)} %cov_ref.1), custom_call_target="tpu_custom_call" | custom-call | flops 8000000000 | bytes 12000000 | tf_op jit(solution)/shard_map/pallas_call | solution.py:395
  90.0 0.0 copy-done
  90.0 1.8 %fusion = f32[128,640]{1,0:T(8,128)} fusion(f32[128,640]{1,0:T(8,128)} %shard_map.73, s32[640]{0:T(1024)S(1)} %select_bitcast_fusion, s32[640]{0:T(1024)S(1)} %pad_dynamic-slice_fusion, s32[128]{0:T(128)S(1)} %copy-done), kind=kLoop, calls=%fused_computation.1 | loop fusion | flops 327680 | bytes 660992 | tf_op jit(solution)/shard_map/jit(_where)/select_n | solution.py:429
  (1 shorter events, 0.0 us)
Async XLA Ops:
  2.2 87.7 %copy-start = (s32[128]{0:T(128)S(1)}, s32[128]{0:T(128)}, u32[]{:S(2)}) copy-start(s32[128]{0:T(128)} %param.13) | copy-start | bytes 1540

commit v3 on v2

--- a/solution.py
+++ b/solution.py
@@ -167,7 +167,9 @@
         pl.semaphore_signal(barrier, inc=1, device_id={"sample": peer(d)}, device_id_type=MESH)
     pl.semaphore_wait(barrier, len(near) + 3)
 
-    @pl.loop(0, PARTS)
+    ahead = 3
+
+    @pl.loop(0, ahead)
     def _(k):
         x_copy(k).start()
 
@@ -176,6 +178,8 @@
     def onto(k):
         x_copy(k).wait_recv()
         y_copy(k).start()
+        if k + ahead < PARTS:
+            x_copy(k + ahead).start()
 
     basis[...] = jnp.zeros_like(basis)
     base[...] = jnp.zeros_like(base)

time: 92 us -> 86.8 us (0.943)
  Pallas kernels: 87.7 us -> 82.5 us
    pallas_call x1, Pallas kernels: 87.7 us -> 82.5 us  [scan(): pl.pallas_call(functools.partial(scan_kernel, ncov, scale), out_shape=blo...]
where the time goes in v3:
time: 86.8 us; the launch traced here: 86.6 us
  Pallas kernels  82.5 us (95%)
  other arithmetic  1.92 us (2%)
  local copies, waits for them, and re-layouts  1.51 us (2%)
    pallas_call x1, Pallas kernels, scan(): pl.pallas_call(functools.partial(scan_kernel, ncov, scale), out_shape=blo...  82.5 us
    select_n x1, other arithmetic, fused(): return jnp.where(tested, value, jnp.float32(0.0))  1.83 us

profile of v3, /device:TPU:0, one launch (start us, length us, event | category | flops | bytes accessed | tf_op | source)
XLA Modules:
  0.0 86.6 jit_solution(9519018676557351959)
XLA Ops:
  0.7 0.7 pad_dynamic-slice_fusion.1
  1.4 0.1 select_bitcast_fusion
  1.5 0.8 pad_dynamic-slice_fusion
  2.2 0.0 copy-start
  2.2 82.5 %shard_map.73 = f32[128,640]{1,0:T(8,128)} custom-call(bf16[8192,512]{1,0:T(8,128)(2,1)} %geno_hbm.1, bf16[8192,128]{1,0:T(8,128)(2,1)} %probe_hbm.1, f32[20,8192]{1,0:T(8,128)} %cov_ref.1), custom_call_target="tpu_custom_call" | custom-call | flops 8000000000 | bytes 12000000 | tf_op jit(solution)/shard_map/pallas_call | solution.py:399
  84.8 0.0 copy-done
  84.8 1.8 %fusion = f32[128,640]{1,0:T(8,128)} fusion(f32[128,640]{1,0:T(8,128)} %shard_map.73, s32[640]{0:T(1024)S(1)} %select_bitcast_fusion, s32[640]{0:T(1024)S(1)} %pad_dynamic-slice_fusion, s32[128]{0:T(128)S(1)} %copy-done), kind=kLoop, calls=%fused_computation.1 | loop fusion | flops 327680 | bytes 660992 | tf_op jit(solution)/shard_map/jit(_where)/select_n | solution.py:433
  (1 shorter events, 0.0 us)
Async XLA Ops:
  2.2 82.5 %copy-start = (s32[128]{0:T(128)S(1)}, s32[128]{0:T(128)}, u32[]{:S(2)}) copy-start(s32[128]{0:T(128)} %param.13) | copy-start | bytes 1540
